TPU v7x, 128 devices: a whole 4x4x4 slice. The times are simulated.
128 devices in a mesh: lon: 8 (over y, core), lat: 16 (over z, x).
Axes of the slice: x: 4, y: 4, z: 4, core: 2. Of those that a mesh axis runs over, the one named last changes fastest.
Arguments:
- state: float32 [512, 4, 16, 2880], P('lat', None, None, 'lon'), may hold values from -6 to 6
- band: int32 [256], replicated, may hold values from 1 to 32, as said below
- damping: float32 [256], replicated, may hold values from 0.2 to 0.9
Outputs:
- advanced: float32 [512, 4, 16, 2880], P('lat', None, None, 'lon')
Inputs may be any that keep to these rules, and one draw needn't show every extreme that they name: Each polar latitude's band half width is an integer from 1 to 32; 32 is reached at some latitude.
All inputs are finite; a program needn't handle non-finite values.
Results may differ from a plain program's by a relative error of at most 0.00007.
Values sent between devices are 32-bit elements; how exact they have to be, the bound alone decides.
A program may use at most 128 MiB of HBM per device.

v0:
```python
import math
import jax
import jax.numpy as jnp
from jax import lax
from jax.sharding import PartitionSpec as P

MAXB = 32
KX = 0.004
KY = 0.1
FC = 0.2
GROUP = 5


def with_halo(cells, sides, width, closed):
    for axis, dim in sides:
        count = lax.axis_size(axis)
        ends = count if closed else count - 1
        head = lax.slice_in_dim(cells, 0, width, axis=dim)
        tail = lax.slice_in_dim(cells, cells.shape[dim] - width, cells.shape[dim], axis=dim)
        cells = jnp.concatenate(
            [
                lax.ppermute(tail, axis, [(i, (i + 1) % count) for i in range(ends)]),
                cells,
                lax.ppermute(head, axis, [((i + 1) % count, i) for i in range(ends)]),
            ],
            axis=dim,
        )
    return cells


def advance_cells(padded, cos_rows, sin_rows, cos_pad):
    u = padded[:, 0]
    v = padded[:, 1]
    h = padded[:, 2]
    q = padded[:, 3]
    inv = 1.0 / cos_rows[:, None, None]
    sn = sin_rows[:, None, None]
    cp = cos_pad[:, None, None]

    def middle(a):
        return a[1:-1, :, 1:-1]

    def east(a):
        return a[1:-1, :, 2:]

    def west(a):
        return a[1:-1, :, :-2]

    def north(a):
        return a[2:, :, 1:-1]

    def south(a):
        return a[:-2, :, 1:-1]

    flux_x = u * h
    flux_y = v * h * cp
    h_new = (
        middle(h)
        - KX * inv * (east(flux_x) - west(flux_x))
        - KY * inv * (north(flux_y) - south(flux_y))
    )
    u_new = middle(u) - KX * inv * (east(h) - west(h)) + FC * sn * middle(v)
    v_new = middle(v) - KY * (north(h) - south(h)) - FC * sn * middle(u)
    q_new = (
        middle(q)
        - KX * inv * middle(u) * (east(q) - west(q))
        - KY * middle(v) * (north(q) - south(q))
    )
    return jnp.stack([u_new, v_new, h_new, q_new], axis=1)


def tap_smooth(extended, width, length):
    taps = jnp.arange(-MAXB, MAXB + 1).astype(jnp.float32)
    weights = (
        jnp.maximum(width[:, None] + 1.0 - jnp.abs(taps)[None, :], 0.0)
        / (width[:, None] + 1.0) ** 2
    )
    start_shape = extended.shape[:3] + (length,)
    tap_count = 2 * MAXB + 1
    turns = tap_count // GROUP

    def add_one(tap, total):
        weight = lax.dynamic_index_in_dim(weights, tap, 1, keepdims=False)
        return total + weight[:, None, None, None] * lax.dynamic_slice_in_dim(
            extended, tap, length, 3
        )

    def add_group(step, total):
        for offset in range(GROUP):
            total = add_one(step * GROUP + offset, total)
        return total

    total = lax.fori_loop(0, turns, add_group, jnp.zeros(start_shape, jnp.float32))
    return total


def shards(state, band, damping):
    lon_count = lax.axis_size("lon")
    lat_count = lax.axis_size("lat")
    lat_rows, field_count, levels, lon_cells = state.shape
    lon_total = lon_cells * lon_count
    lat_total = lat_rows * lat_count
    polar_total = lat_total // 2
    quarter = lat_total // 4
    lon_place = lax.axis_index("lon")
    lat_place = lax.axis_index("lat")
    rimmed = with_halo(state, (("lon", 3),), 1, True)
    padded = with_halo(rimmed, (("lat", 0),), 1, False)
    rows = lat_place * lat_rows + jnp.arange(-1, lat_rows + 1, dtype=jnp.int32)
    angle = math.pi * ((rows.astype(jnp.float32) + 0.5) / lat_total - 0.5)
    cos_pad = jnp.cos(angle)
    stepped = advance_cells(padded, cos_pad[1:-1], jnp.sin(angle[1:-1]), cos_pad)
    band_float = band.astype(jnp.float32)

    def row_params(lats):
        is_polar = (lats < quarter) | (lats >= 3 * quarter)
        polar_place = jnp.where(lats < quarter, lats, lats - polar_total)
        onehot = (
            (polar_place[:, None] == jnp.arange(polar_total, dtype=jnp.int32)[None, :])
            & is_polar[:, None]
        ).astype(jnp.float32)
        width = jnp.dot(onehot, band_float, precision=lax.Precision.HIGHEST)
        strength = jnp.dot(onehot, damping, precision=lax.Precision.HIGHEST)
        return (width, strength)

    def damp_block(fields, lats):
        width, strength = row_params(lats)
        extended = jnp.concatenate([fields[..., -MAXB:], fields, fields[..., :MAXB]], axis=3)
        smooth = tap_smooth(extended, width, lon_total)
        return fields + strength[:, None, None, None] * (smooth - fields)

    gathered = lax.all_to_all(stepped, "lon", split_axis=0, concat_axis=3, tiled=True)
    part_rows = gathered.shape[0]
    spread = lax.all_to_all(gathered, "lat", split_axis=2, concat_axis=0, tiled=True)
    slots = jnp.arange(lat_count * part_rows, dtype=jnp.int32)
    lats = slots // part_rows * lat_rows + lon_place * part_rows + slots % part_rows
    edge = lat_count // 4 * part_rows
    southern = damp_block(spread[:edge], lats[:edge])
    northern = damp_block(spread[-edge:], lats[-edge:])
    spread = jnp.concatenate([southern, spread[edge:-edge], northern], axis=0)
    damped = lax.all_to_all(spread, "lat", split_axis=0, concat_axis=2, tiled=True)
    return lax.all_to_all(damped, "lon", split_axis=3, concat_axis=0, tiled=True)


def solution(mesh):
    in_specs = (P("lat", None, None, "lon"), P(), P())
    out_specs = P("lat", None, None, "lon")
    return jax.shard_map(shards, mesh=mesh, in_specs=in_specs, out_specs=out_specs, check_vma=False)
```

profile of v0, /device:TPU:1, one launch (start us, length us, event | category | flops | bytes accessed | tf_op | source)
XLA Modules:
  0.0 553.1 jit_solution(18015981450221543756)
XLA Ops:
  29.0 45.6 %all_to_all.69 = f32[32,4,16,360]{3,2,1,0:T(8,128)S(1)} all-to-all(f32[32,4,16,360]{3,2,1,0:T(8,128)S(1)} %pad_maximum_fusion.1), channel_id=1, replica_groups=mesh['lon'=8,'lat'=16] {'lon'}, dimensions={0} | all-to-all | bytes 5898240 | tf_op jit(solution)/shard_map/all_to_all | solution.py:132
  83.1 9.7 %all-to-all-start.1 = ((f32[4,4,16,2880]{3,1,0,2:T(4,128)}), f32[4,4,16,2880]{3,1,0,2:T(4,128)}, u32[]{:S(2)}, u32[]{:S(2)}) async-start(f32[4,4,16,2880]{3,1,0,2:T(4,128)} %copy.80), calls=%async_computation.1 | async-start | bytes 6029312 | tf_op jit(solution)/shard_map/all_to_all | solution.py:134
  94.0 42.7 %all-to-all-done.1 = f32[4,4,16,2880]{3,1,0,2:T(4,128)} async-done(((f32[4,4,16,2880]{3,1,0,2:T(4,128)}), f32[4,4,16,2880]{3,1,0,2:T(4,128)}, u32[]{:S(2)}, u32[]{:S(2)}) %all-to-all-start.1) | async-done | bytes 2949152 | tf_op jit(solution)/shard_map/all_to_all | solution.py:134
  145.2 115.6 %while.32 = (s32[]{:T(128)}, f32[16,4,1,2880]{3,2,1,0:T(1,128)S(1)}, f32[16,65]{0,1:T(8,128)S(1)}, f32[16,4,1,2944]{3,2,1,0:T(1,128)S(1)}, s32[]{:T(128)}, /*ind...) while((s32[]{:T(128)}, ...), condition=%wide.region_1.2_spmd.clone, body=%wide.region_0.1_spmd.clone.sunk | while | flops 2027553 | bytes 5162514 | solution.py:93
  145.3 8.8 %multiply_add_fusion.4 = f32[16,4,1,2880]{3,2,1,0:T(1,128)S(1)} fusion(f32[16,4,1,2944]{3,2,1,0:T(1,128)S(1)} %get-tuple-element.535, s32[]{:T(128)S(6)} %select_n.276, s32[]{:T(128)S(6)} %select_n.277, s32[]{:T(128)S(6)} %select_n.278, s32[]{:T(128)S(6)} %select_n.279, s32[]{:T(128)S(6)} %select_n.280, f32[16,4,1,2880]{3,2,1,0:T(1,128)S(1)} %get-tuple-element.513, ...), kind=kLoop, calls=%fused_computation.4.clone.1 | loop fusion | flops 2027520 | bytes 5161301 | tf_op jit(solution)/shard_map/while/body/eval_jaxpr/add | solution.py:84
  154.1 8.8 %multiply_add_fusion.4 = f32[16,4,1,2880]{3,2,1,0:T(1,128)S(1)} fusion(f32[16,4,1,2944]{3,2,1,0:T(1,128)S(1)} %get-tuple-element.535, s32[]{:T(128)S(6)} %select_n.276, s32[]{:T(128)S(6)} %select_n.277, s32[]{:T(128)S(6)} %select_n.278, s32[]{:T(128)S(6)} %select_n.279, s32[]{:T(128)S(6)} %select_n.280, f32[16,4,1,2880]{3,2,1,0:T(1,128)S(1)} %get-tuple-element.513, ...), kind=kLoop, calls=%fused_computation.4.clone.1 | loop fusion | flops 2027520 | bytes 5161301 | tf_op jit(solution)/shard_map/while/body/eval_jaxpr/add | solution.py:84
  163.0 8.8 %multiply_add_fusion.4 = f32[16,4,1,2880]{3,2,1,0:T(1,128)S(1)} fusion(f32[16,4,1,2944]{3,2,1,0:T(1,128)S(1)} %get-tuple-element.535, s32[]{:T(128)S(6)} %select_n.276, s32[]{:T(128)S(6)} %select_n.277, s32[]{:T(128)S(6)} %select_n.278, s32[]{:T(128)S(6)} %select_n.279, s32[]{:T(128)S(6)} %select_n.280, f32[16,4,1,2880]{3,2,1,0:T(1,128)S(1)} %get-tuple-element.513, ...), kind=kLoop, calls=%fused_computation.4.clone.1 | loop fusion | flops 2027520 | bytes 5161301 | tf_op jit(solution)/shard_map/while/body/eval_jaxpr/add | solution.py:84
  171.9 8.8 %multiply_add_fusion.4 = f32[16,4,1,2880]{3,2,1,0:T(1,128)S(1)} fusion(f32[16,4,1,2944]{3,2,1,0:T(1,128)S(1)} %get-tuple-element.535, s32[]{:T(128)S(6)} %select_n.276, s32[]{:T(128)S(6)} %select_n.277, s32[]{:T(128)S(6)} %select_n.278, s32[]{:T(128)S(6)} %select_n.279, s32[]{:T(128)S(6)} %select_n.280, f32[16,4,1,2880]{3,2,1,0:T(1,128)S(1)} %get-tuple-element.513, ...), kind=kLoop, calls=%fused_computation.4.clone.1 | loop fusion | flops 2027520 | bytes 5161301 | tf_op jit(solution)/shard_map/while/body/eval_jaxpr/add | solution.py:84
  180.8 8.8 %multiply_add_fusion.4 = f32[16,4,1,2880]{3,2,1,0:T(1,128)S(1)} fusion(f32[16,4,1,2944]{3,2,1,0:T(1,128)S(1)} %get-tuple-element.535, s32[]{:T(128)S(6)} %select_n.276, s32[]{:T(128)S(6)} %select_n.277, s32[]{:T(128)S(6)} %select_n.278, s32[]{:T(128)S(6)} %select_n.279, s32[]{:T(128)S(6)} %select_n.280, f32[16,4,1,2880]{3,2,1,0:T(1,128)S(1)} %get-tuple-element.513, ...), kind=kLoop, calls=%fused_computation.4.clone.1 | loop fusion | flops 2027520 | bytes 5161301 | tf_op jit(solution)/shard_map/while/body/eval_jaxpr/add | solution.py:84
  189.7 8.8 %multiply_add_fusion.4 = f32[16,4,1,2880]{3,2,1,0:T(1,128)S(1)} fusion(f32[16,4,1,2944]{3,2,1,0:T(1,128)S(1)} %get-tuple-element.535, s32[]{:T(128)S(6)} %select_n.276, s32[]{:T(128)S(6)} %select_n.277, s32[]{:T(128)S(6)} %select_n.278, s32[]{:T(128)S(6)} %select_n.279, s32[]{:T(128)S(6)} %select_n.280, f32[16,4,1,2880]{3,2,1,0:T(1,128)S(1)} %get-tuple-element.513, ...), kind=kLoop, calls=%fused_computation.4.clone.1 | loop fusion | flops 2027520 | bytes 5161301 | tf_op jit(solution)/shard_map/while/body/eval_jaxpr/add | solution.py:84
  198.6 8.8 %multiply_add_fusion.4 = f32[16,4,1,2880]{3,2,1,0:T(1,128)S(1)} fusion(f32[16,4,1,2944]{3,2,1,0:T(1,128)S(1)} %get-tuple-element.535, s32[]{:T(128)S(6)} %select_n.276, s32[]{:T(128)S(6)} %select_n.277, s32[]{:T(128)S(6)} %select_n.278, s32[]{:T(128)S(6)} %select_n.279, s32[]{:T(128)S(6)} %select_n.280, f32[16,4,1,2880]{3,2,1,0:T(1,128)S(1)} %get-tuple-element.513, ...), kind=kLoop, calls=%fused_computation.4.clone.1 | loop fusion | flops 2027520 | bytes 5161301 | tf_op jit(solution)/shard_map/while/body/eval_jaxpr/add | solution.py:84
  207.5 8.8 %multiply_add_fusion.4 = f32[16,4,1,2880]{3,2,1,0:T(1,128)S(1)} fusion(f32[16,4,1,2944]{3,2,1,0:T(1,128)S(1)} %get-tuple-element.535, s32[]{:T(128)S(6)} %select_n.276, s32[]{:T(128)S(6)} %select_n.277, s32[]{:T(128)S(6)} %select_n.278, s32[]{:T(128)S(6)} %select_n.279, s32[]{:T(128)S(6)} %select_n.280, f32[16,4,1,2880]{3,2,1,0:T(1,128)S(1)} %get-tuple-element.513, ...), kind=kLoop, calls=%fused_computation.4.clone.1 | loop fusion | flops 2027520 | bytes 5161301 | tf_op jit(solution)/shard_map/while/body/eval_jaxpr/add | solution.py:84
  216.4 8.8 %multiply_add_fusion.4 = f32[16,4,1,2880]{3,2,1,0:T(1,128)S(1)} fusion(f32[16,4,1,2944]{3,2,1,0:T(1,128)S(1)} %get-tuple-element.535, s32[]{:T(128)S(6)} %select_n.276, s32[]{:T(128)S(6)} %select_n.277, s32[]{:T(128)S(6)} %select_n.278, s32[]{:T(128)S(6)} %select_n.279, s32[]{:T(128)S(6)} %select_n.280, f32[16,4,1,2880]{3,2,1,0:T(1,128)S(1)} %get-tuple-element.513, ...), kind=kLoop, calls=%fused_computation.4.clone.1 | loop fusion | flops 2027520 | bytes 5161301 | tf_op jit(solution)/shard_map/while/body/eval_jaxpr/add | solution.py:84
  225.3 8.8 %multiply_add_fusion.4 = f32[16,4,1,2880]{3,2,1,0:T(1,128)S(1)} fusion(f32[16,4,1,2944]{3,2,1,0:T(1,128)S(1)} %get-tuple-element.535, s32[]{:T(128)S(6)} %select_n.276, s32[]{:T(128)S(6)} %select_n.277, s32[]{:T(128)S(6)} %select_n.278, s32[]{:T(128)S(6)} %select_n.279, s32[]{:T(128)S(6)} %select_n.280, f32[16,4,1,2880]{3,2,1,0:T(1,128)S(1)} %get-tuple-element.513, ...), kind=kLoop, calls=%fused_computation.4.clone.1 | loop fusion | flops 2027520 | bytes 5161301 | tf_op jit(solution)/shard_map/while/body/eval_jaxpr/add | solution.py:84
  234.2 8.8 %multiply_add_fusion.4 = f32[16,4,1,2880]{3,2,1,0:T(1,128)S(1)} fusion(f32[16,4,1,2944]{3,2,1,0:T(1,128)S(1)} %get-tuple-element.535, s32[]{:T(128)S(6)} %select_n.276, s32[]{:T(128)S(6)} %select_n.277, s32[]{:T(128)S(6)} %select_n.278, s32[]{:T(128)S(6)} %select_n.279, s32[]{:T(128)S(6)} %select_n.280, f32[16,4,1,2880]{3,2,1,0:T(1,128)S(1)} %get-tuple-element.513, ...), kind=kLoop, calls=%fused_computation.4.clone.1 | loop fusion | flops 2027520 | bytes 5161301 | tf_op jit(solution)/shard_map/while/body/eval_jaxpr/add | solution.py:84
  243.0 8.8 %multiply_add_fusion.4 = f32[16,4,1,2880]{3,2,1,0:T(1,128)S(1)} fusion(f32[16,4,1,2944]{3,2,1,0:T(1,128)S(1)} %get-tuple-element.535, s32[]{:T(128)S(6)} %select_n.276, s32[]{:T(128)S(6)} %select_n.277, s32[]{:T(128)S(6)} %select_n.278, s32[]{:T(128)S(6)} %select_n.279, s32[]{:T(128)S(6)} %select_n.280, f32[16,4,1,2880]{3,2,1,0:T(1,128)S(1)} %get-tuple-element.513, ...), kind=kLoop, calls=%fused_computation.4.clone.1 | loop fusion | flops 2027520 | bytes 5161301 | tf_op jit(solution)/shard_map/while/body/eval_jaxpr/add | solution.py:84
  264.3 115.6 %while.33 = (s32[]{:T(128)}, f32[16,4,1,2880]{3,2,1,0:T(1,128)S(1)}, f32[16,65]{0,1:T(8,128)S(1)}, f32[16,4,1,2944]{3,2,1,0:T(1,128)S(1)}, s32[]{:T(128)}, /*ind...) while((s32[]{:T(128)}, ...), condition=%wide.region_3.4_spmd.clone, body=%wide.region_2.3_spmd.clone.sunk | while | flops 2027553 | bytes 5162514 | solution.py:93
  382.4 39.4 %all_to_all.70 = f32[64,4,1,2880]{3,1,2,0:T(4,128)S(1)} all-to-all(f32[64,4,1,2880]{3,1,2,0:T(4,128)S(1)} %maximum_bitcast_fusion), channel_id=1, replica_groups=mesh['lon'=8,'lat'=16] {'lat'}, dimensions={0} | all-to-all | bytes 5898240 | tf_op jit(solution)/shard_map/all_to_all | solution.py:141
  421.9 15.9 %copy.86 = f32[4,4,16,2880]{2,1,0,3:T(4,128)} copy(f32[4,4,16,2880]{3,1,0,2:T(4,128)S(1)} %bitcast.106) | data formatting | bytes 5898240 | tf_op jit(solution)/shard_map/all_to_all | solution.py:141
  437.8 19.6 %reshape.143 = f32[8,1,92160]{2,1,0:T(1,128)S(1)} reshape(f32[2880,4,4,16]{3,2,1,0:T(4,128)} %bitcast.102) | data formatting | bytes 5898240
  457.4 43.3 %all_to_all.71 = f32[8,1,92160]{2,1,0:T(1,128)} all-to-all(f32[8,1,92160]{2,1,0:T(1,128)S(1)} %reshape.143), channel_id=1, replica_groups=mesh['lon'=8,'lat'=16] {'lon'}, dimensions={0} | all-to-all | bytes 5898240 | tf_op jit(solution)/shard_map/all_to_all | solution.py:142
  501.2 9.7 %reduce = f32[8,92160]{1,0:T(8,128)S(1)} reduce(f32[8,1,92160]{2,1,0:T(1,128)} %all_to_all.71, f32[]{:T(128)} %broadcast.173), dimensions={1}, to_apply=%all_to_all.61.reduce_sub_computation | reduce | bytes 5898244 | tf_op jit(solution)/shard_map/all_to_all | solution.py:142
  510.9 25.0 %reshape.144 = f32[2880,4,4,16]{3,2,1,0:T(4,128)} reshape(f32[8,92160]{1,0:T(8,128)S(1)} %reduce) | data formatting | bytes 5898240
  535.8 17.1 %copy.90 = f32[4,4,16,8,360]{4,2,1,0,3:T(8,128)} copy(f32[4,4,16,8,360]{2,1,0,4,3:T(4,128)} %bitcast.103) | data formatting | bytes 5898240 | tf_op jit(solution)/shard_map/all_to_all | solution.py:142
  (107 shorter events, 177.2 us)
Async XLA Ops:
  0.0 93.1 %copy-start = (f32[256]{0:T(256)S(1)}, f32[256]{0:T(256)}, u32[]{:S(2)}) copy-start(f32[256]{0:T(256)} %param.9) | copy-start | bytes 3076
  3.2 11.2 %copy-start.2 = (f32[32,4,16,360]{3,2,1,0:T(8,128)S(1)}, f32[32,4,16,360]{3,2,1,0:T(8,128)}, u32[]{:S(2)}) copy-start(f32[32,4,16,360]{3,2,1,0:T(8,128)} %param.7) | copy-start | bytes 8847364
  5.2 7.9 %collective-permute-start.1 = (f32[32,4,16,1]{0,2,3,1:T(8,128)S(1)}, f32[32,4,16,1]{0,2,3,1:T(8,128)S(1)}, u32[]{:S(2)}, u32[]{:S(2)}) collective-permute-start(f32[32,4,16,1]{0,2,3,1:T(8,128)S(1)} %copy.92), channel_id=1, source_target_pairs={{16,0},{32,16},{48,32},{64,48},{80,64},{96,80},{112,96},{0,112},{1... | collective-permute-start | bytes 24584 | tf_op jit(solution)/shard_map/ppermute | solution.py:24
  8.4 3.2 collective-permute-start
  14.5 9.6 %copy-start.3 = (f32[32,4,16,1]{3,2,0,1:T(8,128)S(1)}, f32[32,4,16,1]{3,2,0,1:T(8,128)}, u32[]{:S(2)}) copy-start(f32[32,4,16,1]{3,2,0,1:T(8,128)} %copy.73) | copy-start | bytes 24580
  14.5 9.6 %copy-start.4 = (f32[32,4,16,1]{3,2,0,1:T(8,128)S(1)}, f32[32,4,16,1]{3,2,0,1:T(8,128)}, u32[]{:S(2)}) copy-start(f32[32,4,16,1]{3,2,0,1:T(8,128)} %copy.75) | copy-start | bytes 24580
  15.6 4.7 collective-permute-start.2
  18.7 5.4 collective-permute-start.3
  83.1 9.7 %copy-start.7 = (s32[256]{0:T(256)S(1)}, s32[256]{0:T(256)}, u32[]{:S(2)}) copy-start(s32[256]{0:T(256)} %param.8) | copy-start | bytes 3076
  83.1 53.6 %all-to-all-start.1 = ((f32[4,4,16,2880]{3,1,0,2:T(4,128)}), f32[4,4,16,2880]{3,1,0,2:T(4,128)}, u32[]{:S(2)}, u32[]{:S(2)}) async-start(f32[4,4,16,2880]{3,1,0,2:T(4,128)} %copy.80), calls=%async_computation.1 | async-start | bytes 6029312 | tf_op jit(solution)/shard_map/all_to_all | solution.py:134
  140.8 0.9 copy-start.5
  379.9 1.9 copy-start.6
  535.8 17.1 %copy-start.1 = (f32[256]{0:T(256)S(1)}, f32[256]{0:T(256)}, u32[]{:S(2)}) copy-start(f32[256]{0:T(256)} %param.9) | copy-start | bytes 3076
where the time goes:
time: 562 us; the launch traced here: 553 us
  other arithmetic  247 us (44%)
  blocking collectives  128 us (23%)
  local copies, waits for them, and re-layouts  109 us (19%)
  waiting for transfers between devices  48.5 us (9%)
  starting transfers between devices  16.8 us (3%)
    add x26, other arithmetic, add_one(): total + weight[:, None, None, None] * lax.dynamic_slice_in_dim(extended,...  229 us
    unnamed x22, local copies, waits for them, and re-layouts  52.8 us
    all_to_all x1, blocking collectives, shards(): lax.all_to_all(stepped, 'lon', split_axis=0, concat_axis=3, tiled=True)  45.6 us
    all_to_all x1, blocking collectives, shards(): lax.all_to_all(damped, 'lon', split_axis=3, concat_axis=0, tiled=True)  43.3 us
    all_to_all x1, waiting for transfers between devices, shards(): lax.all_to_all(gathered, 'lat', split_axis=2, concat_axis=0, tiled=True)  42.7 us
    all_to_all x1, blocking collectives, shards(): lax.all_to_all(spread, 'lat', split_axis=0, concat_axis=2, tiled=True)  39.4 us
    all_to_all x2, local copies, waits for them, and re-layouts, shards(): lax.all_to_all(damped, 'lon', split_axis=3, concat_axis=0, tiled=True)  17.6 us
    all_to_all x1, local copies, waits for them, and re-layouts, shards(): lax.all_to_all(spread, 'lat', split_axis=0, concat_axis=2, tiled=True)  15.9 us
  transfers between devices with their start and end apart: 5, of which 4 were waited for; matrix products, arithmetic and copies ran while one was open for 1% of the time, Pallas kernels for 0%

commit v1 on v0

--- a/solution.py
+++ b/solution.py
@@ -138,7 +138,10 @@
     southern = damp_block(spread[:edge], lats[:edge])
     northern = damp_block(spread[-edge:], lats[-edge:])
     spread = jnp.concatenate([southern, spread[edge:-edge], northern], axis=0)
-    damped = lax.all_to_all(spread, "lat", split_axis=0, concat_axis=2, tiled=True)
+    damped = jnp.concatenate(
+        lax.all_to_all(jnp.stack(jnp.split(spread, lax.axis_size("lat"), axis=0)), "lat", 0, 0),
+        axis=2,
+    )
     return lax.all_to_all(damped, "lon", split_axis=3, concat_axis=0, tiled=True)
 
 

time: 562 us -> 558 us (level)
    reshape x0 -> x1, local copies, waits for them, and re-layouts: none -> 16 us  [shards(): jnp.concatenate(lax.all_to_all(jnp.stack(jnp.split(spread, lax.axis_size(...]
    all_to_all x1 -> x0, local copies, waits for them, and re-layouts: 15.9 us -> none  [shards(): lax.all_to_all(spread, 'lat', split_axis=0, concat_axis=2, tiled=True)]
    unnamed x22 -> x28, local copies, waits for them, and re-layouts: 52.8 us -> 54.7 us
where the time goes in v1:
time: 558 us; the launch traced here: 549 us
  other arithmetic  246 us (44%)
  blocking collectives  128 us (23%)
  local copies, waits for them, and re-layouts  106 us (19%)
  waiting for transfers between devices  48.5 us (9%)
  starting transfers between devices  16.8 us (3%)
    add x26, other arithmetic, add_one(): total + weight[:, None, None, None] * lax.dynamic_slice_in_dim(extended,...  229 us
    unnamed x28, local copies, waits for them, and re-layouts  54.7 us
    all_to_all x1, blocking collectives, shards(): lax.all_to_all(stepped, 'lon', split_axis=0, concat_axis=3, tiled=True)  45.6 us
    all_to_all x1, blocking collectives, shards(): lax.all_to_all(damped, 'lon', split_axis=3, concat_axis=0, tiled=True)  43.3 us
    all_to_all x1, waiting for transfers between devices, shards(): lax.all_to_all(gathered, 'lat', split_axis=2, concat_axis=0, tiled=True)  42.7 us
    all_to_all x1, blocking collectives, shards(): lax.all_to_all(jnp.stack(jnp.split(spread, lax.axis_size('lat'), axis=0))...  39.4 us
    all_to_all x2, local copies, waits for them, and re-layouts, shards(): lax.all_to_all(damped, 'lon', split_axis=3, concat_axis=0, tiled=True)  17.6 us
    reshape x1, local copies, waits for them, and re-layouts, shards(): jnp.concatenate(lax.all_to_all(jnp.stack(jnp.split(spread, lax.axis_size(...  16 us
  transfers between devices with their start and end apart: 5, of which 4 were waited for; matrix products, arithmetic and copies ran while one was open for 1% of the time, Pallas kernels for 0%

profile of v1, /device:TPU:1, one launch (start us, length us, event | category | flops | bytes accessed | tf_op | source)
XLA Modules:
  0.0 549.3 jit_solution(12398925958732622388)
XLA Ops:
  29.0 45.6 %all_to_all.56 = f32[32,4,16,360]{3,2,1,0:T(8,128)S(1)} all-to-all(f32[32,4,16,360]{3,2,1,0:T(8,128)S(1)} %pad_maximum_fusion.1), channel_id=1, replica_groups=mesh['lon'=8,'lat'=16] {'lon'}, dimensions={0} | all-to-all | bytes 5898240 | tf_op jit(solution)/shard_map/all_to_all | solution.py:132
  79.7 9.7 %all-to-all-start.1 = ((f32[4,4,16,2880]{3,1,0,2:T(4,128)}), f32[4,4,16,2880]{3,1,0,2:T(4,128)}, u32[]{:S(2)}, u32[]{:S(2)}) async-start(f32[4,4,16,2880]{3,1,0,2:T(4,128)} %all_to_all.43), calls=%async_computation.1 | async-start | bytes 6029312 | tf_op jit(solution)/shard_map/all_to_all | solution.py:134
  90.5 42.7 %all-to-all-done.1 = f32[4,4,16,2880]{3,1,0,2:T(4,128)} async-done(((f32[4,4,16,2880]{3,1,0,2:T(4,128)}), f32[4,4,16,2880]{3,1,0,2:T(4,128)}, u32[]{:S(2)}, u32[]{:S(2)}) %all-to-all-start.1) | async-done | bytes 2949152 | tf_op jit(solution)/shard_map/all_to_all | solution.py:134
  139.3 115.6 %while.33 = (s32[]{:T(128)}, f32[16,4,1,2880]{3,2,1,0:T(1,128)S(1)}, f32[16,65]{0,1:T(8,128)S(1)}, f32[16,4,1,2944]{3,2,1,0:T(1,128)S(1)}, s32[]{:T(128)}, /*ind...) while((s32[]{:T(128)}, ...), condition=%wide.region_3.4_spmd.clone, body=%wide.region_2.3_spmd.clone.sunk | while | flops 2027553 | bytes 5162514 | solution.py:93
  139.4 8.8 %multiply_add_fusion.5 = f32[16,4,1,2880]{3,2,1,0:T(1,128)S(1)} fusion(f32[16,4,1,2944]{3,2,1,0:T(1,128)S(1)} %get-tuple-element.511, s32[]{:T(128)S(6)} %select_n.286, s32[]{:T(128)S(6)} %select_n.287, s32[]{:T(128)S(6)} %select_n.288, s32[]{:T(128)S(6)} %select_n.289, s32[]{:T(128)S(6)} %select_n.290, ...), kind=kLoop, calls=%fused_computation.19.clone.1 | loop fusion | flops 2027520 | bytes 5161301 | tf_op jit(solution)/shard_map/while/body/eval_jaxpr/add | solution.py:84
  148.2 8.8 %multiply_add_fusion.5 = f32[16,4,1,2880]{3,2,1,0:T(1,128)S(1)} fusion(f32[16,4,1,2944]{3,2,1,0:T(1,128)S(1)} %get-tuple-element.511, s32[]{:T(128)S(6)} %select_n.286, s32[]{:T(128)S(6)} %select_n.287, s32[]{:T(128)S(6)} %select_n.288, s32[]{:T(128)S(6)} %select_n.289, s32[]{:T(128)S(6)} %select_n.290, ...), kind=kLoop, calls=%fused_computation.19.clone.1 | loop fusion | flops 2027520 | bytes 5161301 | tf_op jit(solution)/shard_map/while/body/eval_jaxpr/add | solution.py:84
  157.1 8.8 %multiply_add_fusion.5 = f32[16,4,1,2880]{3,2,1,0:T(1,128)S(1)} fusion(f32[16,4,1,2944]{3,2,1,0:T(1,128)S(1)} %get-tuple-element.511, s32[]{:T(128)S(6)} %select_n.286, s32[]{:T(128)S(6)} %select_n.287, s32[]{:T(128)S(6)} %select_n.288, s32[]{:T(128)S(6)} %select_n.289, s32[]{:T(128)S(6)} %select_n.290, ...), kind=kLoop, calls=%fused_computation.19.clone.1 | loop fusion | flops 2027520 | bytes 5161301 | tf_op jit(solution)/shard_map/while/body/eval_jaxpr/add | solution.py:84
  166.0 8.8 %multiply_add_fusion.5 = f32[16,4,1,2880]{3,2,1,0:T(1,128)S(1)} fusion(f32[16,4,1,2944]{3,2,1,0:T(1,128)S(1)} %get-tuple-element.511, s32[]{:T(128)S(6)} %select_n.286, s32[]{:T(128)S(6)} %select_n.287, s32[]{:T(128)S(6)} %select_n.288, s32[]{:T(128)S(6)} %select_n.289, s32[]{:T(128)S(6)} %select_n.290, ...), kind=kLoop, calls=%fused_computation.19.clone.1 | loop fusion | flops 2027520 | bytes 5161301 | tf_op jit(solution)/shard_map/while/body/eval_jaxpr/add | solution.py:84
  174.9 8.8 %multiply_add_fusion.5 = f32[16,4,1,2880]{3,2,1,0:T(1,128)S(1)} fusion(f32[16,4,1,2944]{3,2,1,0:T(1,128)S(1)} %get-tuple-element.511, s32[]{:T(128)S(6)} %select_n.286, s32[]{:T(128)S(6)} %select_n.287, s32[]{:T(128)S(6)} %select_n.288, s32[]{:T(128)S(6)} %select_n.289, s32[]{:T(128)S(6)} %select_n.290, ...), kind=kLoop, calls=%fused_computation.19.clone.1 | loop fusion | flops 2027520 | bytes 5161301 | tf_op jit(solution)/shard_map/while/body/eval_jaxpr/add | solution.py:84
  183.8 8.8 %multiply_add_fusion.5 = f32[16,4,1,2880]{3,2,1,0:T(1,128)S(1)} fusion(f32[16,4,1,2944]{3,2,1,0:T(1,128)S(1)} %get-tuple-element.511, s32[]{:T(128)S(6)} %select_n.286, s32[]{:T(128)S(6)} %select_n.287, s32[]{:T(128)S(6)} %select_n.288, s32[]{:T(128)S(6)} %select_n.289, s32[]{:T(128)S(6)} %select_n.290, ...), kind=kLoop, calls=%fused_computation.19.clone.1 | loop fusion | flops 2027520 | bytes 5161301 | tf_op jit(solution)/shard_map/while/body/eval_jaxpr/add | solution.py:84
  192.7 8.8 %multiply_add_fusion.5 = f32[16,4,1,2880]{3,2,1,0:T(1,128)S(1)} fusion(f32[16,4,1,2944]{3,2,1,0:T(1,128)S(1)} %get-tuple-element.511, s32[]{:T(128)S(6)} %select_n.286, s32[]{:T(128)S(6)} %select_n.287, s32[]{:T(128)S(6)} %select_n.288, s32[]{:T(128)S(6)} %select_n.289, s32[]{:T(128)S(6)} %select_n.290, ...), kind=kLoop, calls=%fused_computation.19.clone.1 | loop fusion | flops 2027520 | bytes 5161301 | tf_op jit(solution)/shard_map/while/body/eval_jaxpr/add | solution.py:84
  201.6 8.8 %multiply_add_fusion.5 = f32[16,4,1,2880]{3,2,1,0:T(1,128)S(1)} fusion(f32[16,4,1,2944]{3,2,1,0:T(1,128)S(1)} %get-tuple-element.511, s32[]{:T(128)S(6)} %select_n.286, s32[]{:T(128)S(6)} %select_n.287, s32[]{:T(128)S(6)} %select_n.288, s32[]{:T(128)S(6)} %select_n.289, s32[]{:T(128)S(6)} %select_n.290, ...), kind=kLoop, calls=%fused_computation.19.clone.1 | loop fusion | flops 2027520 | bytes 5161301 | tf_op jit(solution)/shard_map/while/body/eval_jaxpr/add | solution.py:84
  210.5 8.8 %multiply_add_fusion.5 = f32[16,4,1,2880]{3,2,1,0:T(1,128)S(1)} fusion(f32[16,4,1,2944]{3,2,1,0:T(1,128)S(1)} %get-tuple-element.511, s32[]{:T(128)S(6)} %select_n.286, s32[]{:T(128)S(6)} %select_n.287, s32[]{:T(128)S(6)} %select_n.288, s32[]{:T(128)S(6)} %select_n.289, s32[]{:T(128)S(6)} %select_n.290, ...), kind=kLoop, calls=%fused_computation.19.clone.1 | loop fusion | flops 2027520 | bytes 5161301 | tf_op jit(solution)/shard_map/while/body/eval_jaxpr/add | solution.py:84
  219.4 8.8 %multiply_add_fusion.5 = f32[16,4,1,2880]{3,2,1,0:T(1,128)S(1)} fusion(f32[16,4,1,2944]{3,2,1,0:T(1,128)S(1)} %get-tuple-element.511, s32[]{:T(128)S(6)} %select_n.286, s32[]{:T(128)S(6)} %select_n.287, s32[]{:T(128)S(6)} %select_n.288, s32[]{:T(128)S(6)} %select_n.289, s32[]{:T(128)S(6)} %select_n.290, ...), kind=kLoop, calls=%fused_computation.19.clone.1 | loop fusion | flops 2027520 | bytes 5161301 | tf_op jit(solution)/shard_map/while/body/eval_jaxpr/add | solution.py:84
  228.3 8.8 %multiply_add_fusion.5 = f32[16,4,1,2880]{3,2,1,0:T(1,128)S(1)} fusion(f32[16,4,1,2944]{3,2,1,0:T(1,128)S(1)} %get-tuple-element.511, s32[]{:T(128)S(6)} %select_n.286, s32[]{:T(128)S(6)} %select_n.287, s32[]{:T(128)S(6)} %select_n.288, s32[]{:T(128)S(6)} %select_n.289, s32[]{:T(128)S(6)} %select_n.290, ...), kind=kLoop, calls=%fused_computation.19.clone.1 | loop fusion | flops 2027520 | bytes 5161301 | tf_op jit(solution)/shard_map/while/body/eval_jaxpr/add | solution.py:84
  246.1 8.8 %multiply_add_fusion.5 = f32[16,4,1,2880]{3,2,1,0:T(1,128)S(1)} fusion(f32[16,4,1,2944]{3,2,1,0:T(1,128)S(1)} %get-tuple-element.511, s32[]{:T(128)S(6)} %select_n.286, s32[]{:T(128)S(6)} %select_n.287, s32[]{:T(128)S(6)} %select_n.288, s32[]{:T(128)S(6)} %select_n.289, s32[]{:T(128)S(6)} %select_n.290, ...), kind=kLoop, calls=%fused_computation.19.clone.1 | loop fusion | flops 2027520 | bytes 5161301 | tf_op jit(solution)/shard_map/while/body/eval_jaxpr/add | solution.py:84
  259.3 115.6 %while.32 = (s32[]{:T(128)}, f32[16,4,1,2880]{3,2,1,0:T(1,128)S(1)}, f32[16,65]{0,1:T(8,128)S(1)}, f32[16,4,1,2944]{3,2,1,0:T(1,128)S(1)}, s32[]{:T(128)}, /*ind...) while((s32[]{:T(128)}, ...), condition=%wide.region_1.2_spmd.clone, body=%wide.region_0.1_spmd.clone.sunk | while | flops 2027553 | bytes 5162514 | solution.py:93
  378.5 39.4 %all_to_all.57 = f32[16,4,4,1,2880]{4,2,1,3,0:T(4,128)S(1)} all-to-all(f32[16,4,4,1,2880]{4,2,1,3,0:T(4,128)S(1)} %bitcast.153), channel_id=1, replica_groups=mesh['lon'=8,'lat'=16] {'lat'}, dimensions={0} | all-to-all | bytes 5898240 | tf_op jit(solution)/shard_map/all_to_all | solution.py:142
  418.0 16.0 %copy.57 = f32[4,4,16,2880]{2,1,0,3:T(4,128)} copy(f32[4,4,16,2880]{3,1,0,2:T(4,128)S(1)} %bitcast.146) | data formatting | bytes 5898240 | tf_op jit(solution)/shard_map/reshape | solution.py:141
  433.9 19.6 %reshape.167 = f32[8,1,92160]{2,1,0:T(1,128)S(1)} reshape(f32[2880,4,4,16]{3,2,1,0:T(4,128)} %bitcast.143) | data formatting | bytes 5898240
  453.5 43.3 %all_to_all.58 = f32[8,1,92160]{2,1,0:T(1,128)} all-to-all(f32[8,1,92160]{2,1,0:T(1,128)S(1)} %reshape.167), channel_id=1, replica_groups=mesh['lon'=8,'lat'=16] {'lon'}, dimensions={0} | all-to-all | bytes 5898240 | tf_op jit(solution)/shard_map/all_to_all | solution.py:145
  497.3 9.7 %reduce = f32[8,92160]{1,0:T(8,128)S(1)} reduce(f32[8,1,92160]{2,1,0:T(1,128)} %all_to_all.58, f32[]{:T(128)} %broadcast.173), dimensions={1}, to_apply=%all_to_all.48.reduce_sub_computation | reduce | bytes 5898244 | tf_op jit(solution)/shard_map/all_to_all | solution.py:145
  507.0 25.0 %reshape.168 = f32[2880,4,4,16]{3,2,1,0:T(4,128)} reshape(f32[8,92160]{1,0:T(8,128)S(1)} %reduce) | data formatting | bytes 5898240
  532.0 17.1 %copy.61 = f32[4,4,16,8,360]{4,2,1,0,3:T(8,128)} copy(f32[4,4,16,8,360]{2,1,0,4,3:T(4,128)} %bitcast.144) | data formatting | bytes 5898240 | tf_op jit(solution)/shard_map/all_to_all | solution.py:145
  (111 shorter events, 173.3 us)
Async XLA Ops:
  0.0 89.6 %copy-start = (f32[256]{0:T(256)S(1)}, f32[256]{0:T(256)}, u32[]{:S(2)}) copy-start(f32[256]{0:T(256)} %param.9) | copy-start | bytes 3076
  3.2 11.2 %copy-start.2 = (f32[32,4,16,360]{3,2,1,0:T(8,128)S(1)}, f32[32,4,16,360]{3,2,1,0:T(8,128)}, u32[]{:S(2)}) copy-start(f32[32,4,16,360]{3,2,1,0:T(8,128)} %param.7) | copy-start | bytes 8847364
  5.2 7.9 %collective-permute-start.1 = (f32[32,4,16,1]{0,2,3,1:T(8,128)S(1)}, f32[32,4,16,1]{0,2,3,1:T(8,128)S(1)}, u32[]{:S(2)}, u32[]{:S(2)}) collective-permute-start(f32[32,4,16,1]{0,2,3,1:T(8,128)S(1)} %copy.63), channel_id=1, source_target_pairs={{16,0},{32,16},{48,32},{64,48},{80,64},{96,80},{112,96},{0,112},{1... | collective-permute-start | bytes 24584 | tf_op jit(solution)/shard_map/ppermute | solution.py:24
  8.4 3.2 collective-permute-start
  14.5 9.6 %copy-start.3 = (f32[32,4,16,1]{3,2,0,1:T(8,128)S(1)}, f32[32,4,16,1]{3,2,0,1:T(8,128)}, u32[]{:S(2)}) copy-start(f32[32,4,16,1]{3,2,0,1:T(8,128)} %copy.39) | copy-start | bytes 24580
  14.5 9.6 %copy-start.4 = (f32[32,4,16,1]{3,2,0,1:T(8,128)S(1)}, f32[32,4,16,1]{3,2,0,1:T(8,128)}, u32[]{:S(2)}) copy-start(f32[32,4,16,1]{3,2,0,1:T(8,128)} %copy.41) | copy-start | bytes 24580
  15.6 4.7 collective-permute-start.2
  18.7 5.4 collective-permute-start.3
  79.7 9.7 %copy-start.6 = (s32[256]{0:T(256)S(1)}, s32[256]{0:T(256)}, u32[]{:S(2)}) copy-start(s32[256]{0:T(256)} %param.8) | copy-start | bytes 3076
  79.7 53.6 %all-to-all-start.1 = ((f32[4,4,16,2880]{3,1,0,2:T(4,128)}), f32[4,4,16,2880]{3,1,0,2:T(4,128)}, u32[]{:S(2)}, u32[]{:S(2)}) async-start(f32[4,4,16,2880]{3,1,0,2:T(4,128)} %all_to_all.43), calls=%async_computation.1 | async-start | bytes 6029312 | tf_op jit(solution)/shard_map/all_to_all | solution.py:134
  134.7 0.9 copy-start.5
  532.0 17.1 %copy-start.1 = (f32[256]{0:T(256)S(1)}, f32[256]{0:T(256)}, u32[]{:S(2)}) copy-start(f32[256]{0:T(256)} %param.9) | copy-start | bytes 3076
